TPU v7x, 32 devices: a whole 2x2x4 slice. The times are simulated.
32 devices in a mesh: ctx: 16 (over z, y, core), help: 2 (over x).
Axes of the slice: x: 2, y: 2, z: 4, core: 2. Of those that a mesh axis runs over, the one named last changes fastest.
Arguments:
- queries: bfloat16 [2304, 2048], P('ctx', 'help'), may hold values from -18 to 18
- keys: bfloat16 [2304, 2048], P('ctx', 'help'), may hold values from -18 to 18
- values: bfloat16 [2304, 2048], P('ctx', 'help'), may hold values from -6 to 6
- block_pos: int32 [16], replicated, may hold values from 0 to 15, each once
- w_out: bfloat16 [2048, 2048], P('help'), may hold values from -0.125 to 0.125
Outputs:
- mixed: bfloat16 [2304, 2048], P(('ctx', 'help'))
Inputs may be any that keep to these rules, and one draw needn't show every extreme that they name: `block_pos`: a permutation: each block place occurs once.
All inputs are finite; a program needn't handle non-finite values.
Results may differ from a plain program's by a relative error of at most 0.009.
Values may be sent and summed in bfloat16 or wider, within the bound.
A program may use at most 64 MiB of HBM per device.

v0:
```python
import jax
import jax.numpy as jnp
from jax import lax
from jax.sharding import PartitionSpec as P

HEAD_DIM = 128


def body(queries, keys, values, block_pos, w_out):
    n_ctx = lax.axis_size("ctx")
    device = lax.axis_index("ctx")
    rows = queries.shape[0]
    width = queries.shape[1]
    heads = width // HEAD_DIM
    scale = 1.0 / HEAD_DIM**0.5
    table_index = jnp.arange(n_ctx, dtype=jnp.int32)
    own_block = jnp.sum(jnp.where(table_index == device, block_pos, 0))
    groups = [(queries, own_block * rows + jnp.arange(rows, dtype=jnp.int32))]
    prepared = [
        (group_q.reshape(group_q.shape[0], heads, HEAD_DIM), group_pos)
        for group_q, group_pos in groups
    ]
    start_state = tuple(
        (
            (
                jnp.full((heads, group_q.shape[0]), -1e30, jnp.float32),
                jnp.zeros((heads, group_q.shape[0]), jnp.float32),
                jnp.zeros((heads, group_q.shape[0], HEAD_DIM), jnp.float32),
            )
            for group_q, group_pos in groups
        )
    )
    whole_keys = lax.all_gather(keys, "ctx", axis=0, tiled=True)
    count = whole_keys.shape[0]
    stored = jnp.arange(count, dtype=jnp.int32)
    owner = stored // rows
    placed = jnp.sum(
        jnp.where(owner[:, None] == table_index[None, :], block_pos[None, :], 0), axis=1
    )
    key_pos = placed * rows + stored % rows
    key_heads = whole_keys.reshape(count, heads, HEAD_DIM)
    value_heads = lax.all_gather(values, "ctx", axis=0, tiled=True).reshape(count, heads, HEAD_DIM)
    updated = []
    for (query_heads, query_pos), state in zip(prepared, start_state):

        def compute(state, query_heads=query_heads, query_pos=query_pos):
            best, total, summed = state
            scores = (
                jnp.einsum(
                    "qhd,khd->hqk", query_heads, key_heads, preferred_element_type=jnp.float32
                )
                * scale
            )
            visible = key_pos[None, None, :] <= query_pos[None, :, None]
            piece_top = jnp.max(jnp.where(visible, scores, -1e30), axis=2)
            new_best = jnp.maximum(best, piece_top)
            weights = jnp.where(visible, jnp.exp(scores - new_best[:, :, None]), 0.0)
            new_total = jnp.sum(weights, axis=2)
            product = jnp.einsum(
                "hqk,khd->hqd",
                weights.astype(jnp.bfloat16),
                value_heads,
                preferred_element_type=jnp.float32,
            )
            return (new_best, new_total, product)

        updated.append(compute(state))
    finals = tuple(updated)
    results = []
    for best, total, summed in finals:
        result = summed / total[:, :, None]
        results.append(
            jnp.transpose(result, (1, 0, 2)).reshape(summed.shape[1], width).astype(jnp.bfloat16)
        )
    attended = results[0]
    return lax.psum_scatter(
        jnp.dot(attended, w_out, preferred_element_type=jnp.float32).astype(jnp.bfloat16),
        "help",
        scatter_dimension=0,
        tiled=True,
    )


def solution(mesh):
    in_specs = (P("ctx", "help"), P("ctx", "help"), P("ctx", "help"), P(), P("help", None))
    out_specs = P(("ctx", "help"), None)
    return jax.shard_map(body, mesh=mesh, in_specs=in_specs, out_specs=out_specs, check_vma=False)
```

profile of v0, /device:TPU:0, one launch (start us, length us, event | category | flops | bytes accessed | tf_op | source)
XLA Modules:
  0.0 156.4 jit_solution(7589732562192535551)
XLA Ops:
  6.5 0.0 copy-start
  6.5 0.0 all-gather.3.cloned.1.call-start
  6.5 0.7 all-gather.3.cloned.1.call-update
  7.3 0.0 all-gather.5.cloned.1.call-start
  7.3 0.7 all-gather.5.cloned.1.call-update
  8.0 0.0 reduce-scatter.2.cloned.1.call-start
  8.1 1.3 fusion.33
  10.0 0.8 select_reduce_fusion.1
  10.8 0.3 broadcast_compare_fusion
  11.1 54.7 %all-gather.3.cloned.1.call-done = bf16[2304,1024]{1,0:T(8,128)(2,1)} async-done(((bf16[144,1024]{1,0:T(8,128)(2,1)}), bf16[2304,1024]{1,0:T(8,128)(2,1)}) %all-gather.3.cloned.1.call-update) | async-done | bytes 4718608 | tf_op jit(solution)/shard_map/all_gather | solution.py:33
  65.8 6.8 %copy.19 = bf16[2304,1024]{0,1:T(8,128)(2,1)} copy(bf16[2304,1024]{1,0:T(8,128)(2,1)} %all-gather.3.cloned.1.call-done) | data formatting | bytes 9437184 | tf_op jit(solution)/shard_map/all_gather | solution.py:33
  72.5 0.0 copy-done
  72.5 5.0 %select_reduce_fusion = (f32[8,144]{1,0:T(8,128)S(1)}, f32[8,144,2304]{2,1,0:T(8,128)S(1)}) fusion(pred[144,2304]{1,0:T(8,128)(4,1)S(1)} %broadcast_compare_fusion, bf16[2304,8,128]{0,2,1:T(8,128)(2,1)} %bitcast.28, bf16[144,1024]{1,0:T(8,128)(2,1)S(1)} %copy-done), kind=kOutput, calls=%fused_computation.1 | convolution fusion | flops 687438720 | bytes 15966720 | tf_op jit(solution)/shard_map/qhd,khd->hqk/dot_general | solution.py:49
  77.5 0.0 copy-start.1
  77.6 4.0 %copy-done.1 = f32[8,144,2304]{2,1,0:T(8,128)} copy-done((f32[8,144,2304]{2,1,0:T(8,128)}, f32[8,144,2304]{2,1,0:T(8,128)S(1)}, u32[]{:S(2)}) %copy-start.1) | copy-done | bytes 10616856
  81.5 2.7 %fusion = f32[8,144]{1,0:T(8,128)S(1)} fusion(f32[8,144,2304]{2,1,0:T(8,128)S(1)} %get-tuple-element.6, f32[8,144]{1,0:T(8,128)S(1)} %broadcast_maximum_fusion, pred[144,2304]{1,0:T(8,128)(4,1)S(1)} %broadcast_compare_fusion), kind=kLoop, calls=%fused_computation.2 | loop fusion | flops 10615680 | bytes 10957824 | tf_op jit(solution)/shard_map/reduce_sum | solution.py:58
  84.2 35.8 %all-gather.5.cloned.1.call-done = bf16[2304,1024]{1,0:T(8,128)(2,1)} async-done(((bf16[144,1024]{1,0:T(8,128)(2,1)}), bf16[2304,1024]{1,0:T(8,128)(2,1)}) %all-gather.5.cloned.1.call-update) | async-done | bytes 4718608 | tf_op jit(solution)/shard_map/all_gather | solution.py:42
  120.0 6.7 %copy.22 = bf16[2304,1024]{0,1:T(8,128)(2,1)} copy(bf16[2304,1024]{1,0:T(8,128)(2,1)} %all-gather.5.cloned.1.call-done) | data formatting | bytes 9437184 | tf_op jit(solution)/shard_map/all_gather | solution.py:42
  126.7 0.0 copy-start.2
  126.7 7.6 %fusion.17 = bf16[8,18,8,128]{3,2,1,0:T(8,128)(2,1)S(1)} fusion(bf16[2304,8,128]{0,2,1:T(8,128)(2,1)} %bitcast.29, f32[8,144,2304]{2,1,0:T(8,128)} %copy-done.1, f32[8,144]{1,0:T(8,128)S(1)} %broadcast_maximum_fusion, pred[144,2304]{1,0:T(8,128)(4,1)S(1)} %broadcast_compare_fusion, f32[144,8]{0,1:T(8,128)S(1)} %bitcast.30), kind=kOutput, calls=%fused_computation.13 | convolution fusion | flops 690388992 | bytes 15971328 | tf_op jit(solution)/shard_map/hqk,khd->hqd/dot_general | solution.py:59
  134.3 0.0 copy-done.2
  134.3 1.6 %convolution_convert_fusion = bf16[144,2048]{1,0:T(8,128)(2,1)} fusion(bf16[1024,2048]{1,0:T(8,128)(2,1)S(1)} %copy-done.2, bf16[8,18,8,128]{3,2,1,0:T(8,128)(2,1)S(1)} %fusion.17), kind=kOutput, calls=%fused_computation.9 | convolution fusion | flops 604274688 | bytes 5079040 | tf_op jit(solution)/shard_map/dot_general | solution.py:77
  135.9 0.0 reduce-scatter.2.cloned.1.call-update
  135.9 14.0 %reduce-scatter.2.cloned.1.call-done = bf16[72,2048]{1,0:T(8,128)(2,1)} async-done(((bf16[144,2048]{1,0:T(8,128)(2,1)}), bf16[72,2048]{1,0:T(8,128)(2,1)}) %reduce-scatter.2.cloned.1.call-update) | async-done | bytes 294928 | tf_op jit(solution)/shard_map/reduce_scatter | solution.py:76
  (4 shorter events, 0.0 us)
Async XLA Ops:
  6.5 66.0 %copy-start = (bf16[144,1024]{1,0:T(8,128)(2,1)S(1)}, bf16[144,1024]{1,0:T(8,128)(2,1)}, u32[]{:S(2)}) copy-start(bf16[144,1024]{1,0:T(8,128)(2,1)} %param.5) | copy-start | bytes 884740
  6.5 59.2 %all-gather.3.cloned.1.call-start = ((), (), s32[]{:S(2)}) async-start(), calls=%async_computation.1 | async-start | bytes 5013504 | tf_op jit(solution)/shard_map/all_gather | solution.py:33
  7.3 112.8 %all-gather.5.cloned.1.call-start = ((), (), s32[]{:S(2)}) async-start(), calls=%async_computation.2 | async-start | bytes 5013504 | tf_op jit(solution)/shard_map/all_gather | solution.py:42
  8.0 141.9 %reduce-scatter.2.cloned.1.call-start = ((), (), s32[]{:S(2)}) async-start(), calls=%async_computation.3 | async-start | bytes 884736 | tf_op jit(solution)/shard_map/reduce_scatter | solution.py:76
  77.5 4.0 %copy-start.1 = (f32[8,144,2304]{2,1,0:T(8,128)}, f32[8,144,2304]{2,1,0:T(8,128)S(1)}, u32[]{:S(2)}) copy-start(f32[8,144,2304]{2,1,0:T(8,128)S(1)} %get-tuple-element.6) | copy-start | bytes 31850500
  126.7 7.6 %copy-start.2 = (bf16[1024,2048]{1,0:T(8,128)(2,1)S(1)}, bf16[1024,2048]{1,0:T(8,128)(2,1)}, u32[]{:S(2)}) copy-start(bf16[1024,2048]{1,0:T(8,128)(2,1)} %param.9) | copy-start | bytes 12582916
Sparse Core Ops, SparseCore 0:
  9.6 56.0 all-gather.2
  68.0 51.9 all-gather.4
  136.0 13.7 reduce-scatter.1
where the time goes:
time: 157 us; the launch traced here: 156 us
  waiting for transfers between devices  106 us (68%)
  local copies, waits for them, and re-layouts  17.5 us (11%)
  matrix products  14.1 us (9%)
  between operations  13.8 us (9%)
  other arithmetic  4.99 us (3%)
    all_gather x1, waiting for transfers between devices, body(): whole_keys = lax.all_gather(keys, 'ctx', axis=0, tiled=True)  54.7 us
    all_gather x1, waiting for transfers between devices, body(): lax.all_gather(values, 'ctx', axis=0, tiled=True)  35.8 us
    reduce_scatter x1, waiting for transfers between devices, body(): lax.psum_scatter(jnp.dot(attended, w_out, preferred_element_type=jnp.floa...  14 us
    dot_general x1, matrix products, compute(): jnp.einsum('hqk,khd->hqd', weights.astype(jnp.bfloat16), value_heads, pre...  7.56 us
    all_gather x1, local copies, waits for them, and re-layouts, body(): whole_keys = lax.all_gather(keys, 'ctx', axis=0, tiled=True)  6.78 us
    all_gather x1, local copies, waits for them, and re-layouts, body(): lax.all_gather(values, 'ctx', axis=0, tiled=True)  6.69 us
    dot_general x1, matrix products, compute(): jnp.einsum('qhd,khd->hqk', query_heads, key_heads, preferred_element_type...  4.98 us
    unnamed x6, local copies, waits for them, and re-layouts  4 us
  transfers between devices with their start and end apart: 3, of which 3 were waited for; matrix products, arithmetic and copies ran while one was open for 11% of the time, Pallas kernels for 0%

commit v1 on v0

v1 whole, which is shorter than its diff:
```python
import functools
import math

import jax
import jax.numpy as jnp
from jax import lax
from jax.experimental import pallas as pl
from jax.experimental.pallas import tpu as pltpu
from jax.sharding import PartitionSpec as P

HEAD_DIM = 128
MESH = pl.DeviceIdType.MESH


def gathered_body(queries, keys, values, block_pos, w_out):
    n_ctx = lax.axis_size("ctx")
    device = lax.axis_index("ctx")
    rows, width = queries.shape
    heads = width // HEAD_DIM
    scale = 1.0 / HEAD_DIM**0.5
    own_block = jnp.sum(jnp.where(jnp.arange(n_ctx) == device, block_pos, 0))
    query_pos = own_block * rows + jnp.arange(rows, dtype=jnp.int32)
    whole_keys = lax.all_gather(keys, "ctx", axis=0, tiled=True)
    whole_values = lax.all_gather(values, "ctx", axis=0, tiled=True)
    count = whole_keys.shape[0]
    key_pos = (block_pos[:, None] * rows + jnp.arange(rows, dtype=jnp.int32)[None, :]).reshape(count)
    query_heads = queries.reshape(rows, heads, HEAD_DIM)
    key_heads = whole_keys.reshape(count, heads, HEAD_DIM)
    value_heads = whole_values.reshape(count, heads, HEAD_DIM)
    scores = (
        jnp.einsum("qhd,khd->hqk", query_heads, key_heads, preferred_element_type=jnp.float32)
        * scale
    )
    visible = key_pos[None, None, :] <= query_pos[None, :, None]
    top = jnp.max(jnp.where(visible, scores, -1e30), axis=2)
    weights = jnp.where(visible, jnp.exp(scores - top[:, :, None]), 0.0)
    total = jnp.sum(weights, axis=2)
    summed = jnp.einsum(
        "hqk,khd->hqd",
        weights.astype(jnp.bfloat16),
        value_heads,
        preferred_element_type=jnp.float32,
    )
    result = summed / total[:, :, None]
    attended = jnp.transpose(result, (1, 0, 2)).reshape(rows, width).astype(jnp.bfloat16)
    return lax.psum_scatter(
        jnp.dot(attended, w_out, preferred_element_type=jnp.float32).astype(jnp.bfloat16),
        "help",
        scatter_dimension=0,
        tiled=True,
    )


def kernel(
    chips, rows, lanes, parts,
    bp_ref, q_hbm, k_hbm, v_hbm, w_hbm, out_ref,
    qbuf, kv, acc, top, total, qpos, osend, att, wbuf, part, psend, precv,
    own_sem, w_sem, q_send, q_recv, kv_send, kv_recv, relay_send, relay_recv,
    o_own, o_send, o_recv, p_send, p_recv,
):
    ctx = lax.axis_index("ctx")
    helper = lax.axis_index("help")
    chip = lax.div(ctx, 2)
    core = lax.rem(ctx, 2)
    sibling = chip * 2 + (1 - core)
    count = chips * rows
    fold = math.log2(math.e) / HEAD_DIM**0.5

    def peer(step):
        return lax.rem(chip + step, chips)

    def head_of(ref, which):
        return ref.at[:, pl.ds(pl.multiple_of(which * HEAD_DIM, HEAD_DIM), HEAD_DIM)]

    def row_block(ref, which):
        return ref.at[pl.ds(pl.multiple_of(which * rows, 16), rows), :]

    w_copy = pltpu.make_async_copy(w_hbm, wbuf, w_sem)
    own = [
        pltpu.make_async_copy(head_of(q_hbm, chip), row_block(qbuf, chip), own_sem.at[0]),
        pltpu.make_async_copy(head_of(k_hbm, chip), kv.at[chip, core, 0], own_sem.at[1]),
        pltpu.make_async_copy(head_of(v_hbm, chip), kv.at[chip, core, 1], own_sem.at[2]),
    ]
    for copy in own:
        copy.start()

    barrier = pltpu.get_barrier_semaphore()
    for step in range(1, chips):
        pl.semaphore_signal(
            barrier, inc=1, device_id=(peer(step) * 2 + core, helper), device_id_type=MESH
        )
    pl.semaphore_signal(barrier, inc=1, device_id=(sibling, helper), device_id_type=MESH)
    pl.semaphore_signal(barrier, inc=1, device_id=(ctx, 1 - helper), device_id_type=MESH)
    pl.semaphore_wait(barrier, chips + 1)

    def q_copy(step, source):
        return pltpu.make_async_remote_copy(
            src_ref=head_of(q_hbm, peer(step)),
            dst_ref=row_block(qbuf, source),
            send_sem=q_send.at[step],
            recv_sem=q_recv.at[source],
            device_id=(peer(step) * 2 + core, helper),
            device_id_type=MESH,
        )

    def kv_copy(step, source, which):
        return pltpu.make_async_remote_copy(
            src_ref=head_of((k_hbm, v_hbm)[which], peer(step)),
            dst_ref=kv.at[source, core, which],
            send_sem=kv_send.at[step, which],
            recv_sem=kv_recv.at[source, which],
            device_id=(peer(step) * 2 + core, helper),
            device_id_type=MESH,
        )

    def relay(source, half):
        return pltpu.make_async_remote_copy(
            src_ref=kv.at[source, half],
            dst_ref=kv.at[source, half],
            send_sem=relay_send.at[source],
            recv_sem=relay_recv.at[source],
            device_id=(sibling, helper),
            device_id_type=MESH,
        )

    for step in range(1, chips):
        q_copy(step, chip).start()
    for step in range(1, chips):
        kv_copy(step, chip, 0).start()
        kv_copy(step, chip, 1).start()
    w_copy.start()

    lane = lax.broadcasted_iota(jnp.int32, (1, count), 1)
    position = jnp.zeros((1, count), jnp.int32)
    for block in range(chips):
        inside = (lane >= block * rows) & (lane < (block + 1) * rows)
        position = jnp.where(
            inside, lane + (bp_ref[block * 2 + core] - block) * rows, position
        )
    qpos[...] = position
    acc[...] = jnp.zeros_like(acc)
    total[...] = jnp.zeros_like(total)
    top[...] = jnp.full(top.shape, -1e9, jnp.float32)

    def attend(source):
        keys = kv[source, :, 0].reshape(2 * rows, HEAD_DIM)
        values = kv[source, :, 1].reshape(2 * rows, HEAD_DIM).T
        first = bp_ref[source * 2] * rows
        second = bp_ref[source * 2 + 1] * rows
        for begin in range(0, count, lanes):
            cols = pl.ds(begin, lanes)
            raw = lax.dot_general(
                keys, qbuf[cols, :], (((1,), (1,)), ((), ())), preferred_element_type=jnp.float32
            )
            inner = lax.broadcasted_iota(jnp.int32, (rows, lanes), 0)
            place = qpos[:, cols]
            raw = jnp.concatenate(
                [
                    jnp.where(inner <= place - first, raw[:rows], -1e30),
                    jnp.where(inner <= place - second, raw[rows:], -1e30),
                ],
                axis=0,
            )
            before = top[:, cols]
            after = jnp.maximum(before, jnp.max(raw, axis=0, keepdims=True))
            weights = jnp.exp2(raw * fold - after * fold)
            keep = jnp.exp2((before - after) * fold)
            top[:, cols] = after
            total[:, cols] = total[:, cols] * keep + jnp.sum(weights, axis=0, keepdims=True)
            acc[:, cols] = acc[:, cols] * keep + jnp.dot(
                values, weights.astype(jnp.bfloat16), preferred_element_type=jnp.float32
            )

    own[1].wait()
    own[2].wait()
    relay(chip, core).start()
    own[0].wait()
    for step in range(1, chips):
        q_copy(step, peer(step)).wait_recv()

    def one_step(step, carry):
        source = peer(step)
        kv_copy(step, source, 0).wait_recv()
        kv_copy(step, source, 1).wait_recv()
        relay(source, core).start()
        done = peer(step - 1)
        relay(done, 1 - core).wait_recv()
        attend(done)
        return carry

    lax.fori_loop(1, chips, one_step, 0)
    last = peer(chips - 1)
    relay(last, 1 - core).wait_recv()
    attend(last)

    def o_copy(block, head):
        return pltpu.make_async_remote_copy(
            src_ref=osend.at[pl.ds(block * rows, rows), :],
            dst_ref=head_of(att, head),
            send_sem=o_send.at[block],
            recv_sem=o_recv.at[head],
            device_id=(block * 2 + core, helper),
            device_id_type=MESH,
        )

    def o_local(block):
        return pltpu.make_async_copy(
            osend.at[pl.ds(block * rows, rows), :], head_of(att, chip), o_own
        )

    sent = 0
    for begin in range(0, count, lanes):
        cols = pl.ds(begin, lanes)
        result = acc[:, cols] * (1.0 / total[:, cols])
        osend[cols, :] = result.T.astype(jnp.bfloat16)
        while (sent + 1) * rows <= begin + lanes:
            block = sent

            @pl.when(chip == block)
            def _():
                o_local(block).start()

            @pl.when(chip != block)
            def _():
                o_copy(block, chip).start()

            sent += 1

    w_copy.wait()
    for block in range(chips):

        @pl.when(chip == block)
        def _():
            o_local(block).wait()

        @pl.when(chip != block)
        def _():
            o_copy(block, block).wait_recv()

    half = rows // 2
    wide = w_hbm.shape[1] // parts

    def p_copy(index):
        return pltpu.make_async_remote_copy(
            src_ref=psend.at[index],
            dst_ref=precv.at[index],
            send_sem=p_send.at[index],
            recv_sem=p_recv.at[index],
            device_id=(ctx, 1 - helper),
            device_id_type=MESH,
        )

    for index in range(parts):
        cols = pl.ds(index * wide, wide)
        part[:, cols] = jnp.dot(att[...], wbuf[:, cols], preferred_element_type=jnp.float32)
        other = part[pl.ds(pl.multiple_of((1 - helper) * half, 8), half), cols]
        fill = jnp.zeros((psend.shape[1] - half, wide), jnp.float32)
        psend[index] = jnp.concatenate([other, fill], axis=0).astype(jnp.bfloat16)
        p_copy(index).start()
    for index in range(parts):
        cols = pl.ds(index * wide, wide)
        p_copy(index).wait_recv()
        mine = part[pl.ds(pl.multiple_of(helper * half, 8), half), cols]
        out_ref[:, cols] = (mine + precv[index].astype(jnp.float32)[:half]).astype(jnp.bfloat16)

    for step in range(1, chips):
        q_copy(step, chip).wait_send()
        kv_copy(step, chip, 0).wait_send()
        kv_copy(step, chip, 1).wait_send()
    for source in range(chips):
        relay(source, core).wait_send()

        @pl.when(chip != source)
        def _():
            o_copy(source, chip).wait_send()

    for index in range(parts):
        p_copy(index).wait_send()


def exchanged_body(chips, queries, keys, values, block_pos, w_out):
    rows, width = queries.shape
    out_width = w_out.shape[1]
    count = chips * rows
    lanes = 384
    parts = 4
    padded = -(-(rows // 2) // 16) * 16
    bf16, f32 = jnp.bfloat16, jnp.float32
    dma = pltpu.SemaphoreType.DMA
    anywhere = pl.BlockSpec(memory_space=pl.ANY)
    return pl.pallas_call(
        functools.partial(kernel, chips, rows, lanes, parts),
        out_shape=jax.ShapeDtypeStruct((rows // 2, out_width), bf16),
        in_specs=[pl.BlockSpec(memory_space=pltpu.SMEM)] + [anywhere] * 4,
        out_specs=pl.BlockSpec(memory_space=pltpu.VMEM),
        scratch_shapes=[
            pltpu.VMEM((count, HEAD_DIM), bf16),
            pltpu.VMEM((chips, 2, 2, rows, HEAD_DIM), bf16),
            pltpu.VMEM((HEAD_DIM, count), f32),
            pltpu.VMEM((1, count), f32),
            pltpu.VMEM((1, count), f32),
            pltpu.VMEM((1, count), jnp.int32),
            pltpu.VMEM((count, HEAD_DIM), bf16),
            pltpu.VMEM((rows, width), bf16),
            pltpu.VMEM((width, out_width), bf16),
            pltpu.VMEM((rows, out_width), f32),
            pltpu.VMEM((parts, padded, out_width // parts), bf16),
            pltpu.VMEM((parts, padded, out_width // parts), bf16),
            dma((3,)),
            dma,
            dma((chips,)),
            dma((chips,)),
            dma((chips, 2)),
            dma((chips, 2)),
            dma((chips,)),
            dma((chips,)),
            dma,
            dma((chips,)),
            dma((chips,)),
            dma((parts,)),
            dma((parts,)),
        ],
        compiler_params=pltpu.CompilerParams(
            collective_id=0, has_side_effects=True, vmem_limit_bytes=40 * 1024 * 1024
        ),
        cost_estimate=pl.CostEstimate(
            flops=8 * count * count * HEAD_DIM + 2 * rows * width * out_width,
            bytes_accessed=2 * (3 * rows * width + width * out_width),
            transcendentals=2 * count * count,
        ),
        name="exchange_attend_project",
    )(block_pos, queries, keys, values, w_out)


def solution(mesh):
    chips = mesh.shape["ctx"] // 2

    def body(queries, keys, values, block_pos, w_out):
        if mesh.shape["help"] == 2 and queries.shape[1] == chips * HEAD_DIM:
            return exchanged_body(chips, queries, keys, values, block_pos, w_out)
        return gathered_body(queries, keys, values, block_pos, w_out)

    in_specs = (P("ctx", "help"), P("ctx", "help"), P("ctx", "help"), P(), P("help", None))
    out_specs = P(("ctx", "help"), None)
    return jax.shard_map(body, mesh=mesh, in_specs=in_specs, out_specs=out_specs, check_vma=False)
```

time: 157 us -> 58 us (0.37)
  waiting for transfers between devices: 106 us -> 0 us
  Pallas kernels: 0 us -> 51.3 us
  matrix products: 14.1 us -> 0 us
  between operations: 13.8 us -> 0.01 us
  local copies, waits for them, and re-layouts: 17.5 us -> 6.44 us
  other arithmetic: 4.99 us -> 0 us
    all_gather x2 -> x0, waiting for transfers between devices: 90.5 us -> none  [the longest x1 54.7 us: body(): whole_keys = lax.all_gather(keys, 'ctx', axis=0, tiled=True)]
    pallas_call x0 -> x1, Pallas kernels: none -> 51.3 us  [exchanged_body(): pl.pallas_call(functools.partial(kernel, chips, rows, lanes, parts), out_...]
    dot_general x3 -> x0, matrix products: 14.1 us -> none  [the longest x1 7.56 us: compute(): jnp.einsum('hqk,khd->hqd', weights.astype(jnp.bfloat16), value_heads, pre...]
    reduce_scatter x1 -> x0, waiting for transfers between devices: 14 us -> none  [body(): lax.psum_scatter(jnp.dot(attended, w_out, preferred_element_type=jnp.floa...]
    all_gather x2 -> x0, local copies, waits for them, and re-layouts: 13.5 us -> none  [the longest x1 6.78 us: body(): whole_keys = lax.all_gather(keys, 'ctx', axis=0, tiled=True)]
    reduce_sum x3 -> x0, other arithmetic: 4.71 us -> none  [the longest x1 2.65 us: compute(): new_total = jnp.sum(weights, axis=2)]
    unnamed x6 -> x11, local copies, waits for them, and re-layouts: 4 us -> 6.44 us
  transfers between devices with their start and end apart: 3 -> 0, of which waited for: 3 -> 0; matrix products, arithmetic and copies ran while one was open for 11% -> 0% of each run, Pallas kernels for 0% -> 0%
where the time goes in v1:
time: 58 us; the launch traced here: 57.8 us
  Pallas kernels  51.3 us (88%)
  local copies, waits for them, and re-layouts  6.44 us (11%)
    pallas_call x1, Pallas kernels, exchanged_body(): pl.pallas_call(functools.partial(kernel, chips, rows, lanes, parts), out_...  51.3 us
    unnamed x11, local copies, waits for them, and re-layouts  6.44 us

profile of v1, /device:TPU:0, one launch (start us, length us, event | category | flops | bytes accessed | tf_op | source)
XLA Modules:
  0.0 57.8 jit_solution(8740608442504287708)
XLA Ops:
  0.0 0.0 copy-start
  0.0 2.2 %copy-done = bf16[1024,2048]{1,0:T(8,128)(2,1)S(1)} copy-done((bf16[1024,2048]{1,0:T(8,128)(2,1)S(1)}, bf16[1024,2048]{1,0:T(8,128)(2,1)}, u32[]{:S(2)}) %copy-start) | copy-done | bytes 4194328
  2.2 0.0 copy-start.1
  2.2 1.0 %copy-done.1 = bf16[144,1024]{1,0:T(8,128)(2,1)S(1)} copy-done((bf16[144,1024]{1,0:T(8,128)(2,1)S(1)}, bf16[144,1024]{1,0:T(8,128)(2,1)}, u32[]{:S(2)}) %copy-start.1) | copy-done | bytes 294936
  3.2 0.0 copy-start.2
  3.2 1.0 %copy-done.2 = bf16[144,1024]{1,0:T(8,128)(2,1)S(1)} copy-done((bf16[144,1024]{1,0:T(8,128)(2,1)S(1)}, bf16[144,1024]{1,0:T(8,128)(2,1)}, u32[]{:S(2)}) %copy-start.2) | copy-done | bytes 294936
  4.1 0.0 copy-start.3
  4.1 1.0 %copy-done.3 = bf16[144,1024]{1,0:T(8,128)(2,1)S(1)} copy-done((bf16[144,1024]{1,0:T(8,128)(2,1)S(1)}, bf16[144,1024]{1,0:T(8,128)(2,1)}, u32[]{:S(2)}) %copy-start.3) | copy-done | bytes 294936
  5.1 0.0 copy-start.4
  5.1 0.7 %copy-done.4 = s32[16]{0:T(128)S(1)} copy-done((s32[16]{0:T(128)S(1)}, s32[16]{0:T(128)}, u32[]{:S(2)}) %copy-start.4) | copy-done | bytes 88
  5.7 51.3 %exchange_attend_project.1 = bf16[72,2048]{1,0:T(8,128)(2,1)S(1)} custom-call(s32[16]{0:T(128)S(1)} %copy-done.4, bf16[144,1024]{1,0:T(8,128)(2,1)S(1)} %copy-done.1, bf16[144,1024]{1,0:T(8,128)(2,1)S(1)} %copy-done.2, bf16[144,1024]{1,0:T(8,128)(2,1)S(1)} %copy-done.3, bf16[1024,2048]{1,0:T(8,128)(2,1)S(1)} %copy-done), custom_call_target="tpu_custom_call" | custom-call | flops 1962934272 | bytes 5079040 | tf_op jit(solution)/shard_map/exchange_attend_project/pallas_call | solution.py:291
  57.0 0.7 %copy.7 = bf16[72,2048]{1,0:T(8,128)(2,1)} copy(bf16[72,2048]{1,0:T(8,128)(2,1)S(1)} %exchange_attend_project.1) | data formatting | bytes 589824
Async XLA Ops:
  0.0 2.2 %copy-start = (bf16[1024,2048]{1,0:T(8,128)(2,1)S(1)}, bf16[1024,2048]{1,0:T(8,128)(2,1)}, u32[]{:S(2)}) copy-start(bf16[1024,2048]{1,0:T(8,128)(2,1)} %w_hbm.1) | copy-start | bytes 12582916
  2.2 1.0 %copy-start.1 = (bf16[144,1024]{1,0:T(8,128)(2,1)S(1)}, bf16[144,1024]{1,0:T(8,128)(2,1)}, u32[]{:S(2)}) copy-start(bf16[144,1024]{1,0:T(8,128)(2,1)} %q_hbm.1) | copy-start | bytes 884740
  3.2 1.0 %copy-start.2 = (bf16[144,1024]{1,0:T(8,128)(2,1)S(1)}, bf16[144,1024]{1,0:T(8,128)(2,1)}, u32[]{:S(2)}) copy-start(bf16[144,1024]{1,0:T(8,128)(2,1)} %k_hbm.1) | copy-start | bytes 884740
  4.1 1.0 %copy-start.3 = (bf16[144,1024]{1,0:T(8,128)(2,1)S(1)}, bf16[144,1024]{1,0:T(8,128)(2,1)}, u32[]{:S(2)}) copy-start(bf16[144,1024]{1,0:T(8,128)(2,1)} %v_hbm.1) | copy-start | bytes 884740
  5.1 0.7 %copy-start.4 = (s32[16]{0:T(128)S(1)}, s32[16]{0:T(128)}, u32[]{:S(2)}) copy-start(s32[16]{0:T(128)} %bp_ref.1) | copy-start | bytes 196

commit v2 on v1

v2 whole, which is shorter than its diff:
```python
import functools
import math

import jax
import jax.numpy as jnp
from jax import lax
from jax.experimental import pallas as pl
from jax.experimental.pallas import tpu as pltpu
from jax.sharding import PartitionSpec as P

HEAD_DIM = 128
MESH = pl.DeviceIdType.MESH


def gathered_body(queries, keys, values, block_pos, w_out):
    n_ctx = lax.axis_size("ctx")
    device = lax.axis_index("ctx")
    rows, width = queries.shape
    heads = width // HEAD_DIM
    scale = 1.0 / HEAD_DIM**0.5
    own_block = jnp.sum(jnp.where(jnp.arange(n_ctx) == device, block_pos, 0))
    query_pos = own_block * rows + jnp.arange(rows, dtype=jnp.int32)
    whole_keys = lax.all_gather(keys, "ctx", axis=0, tiled=True)
    whole_values = lax.all_gather(values, "ctx", axis=0, tiled=True)
    count = whole_keys.shape[0]
    key_pos = (block_pos[:, None] * rows + jnp.arange(rows, dtype=jnp.int32)[None, :]).reshape(count)
    query_heads = queries.reshape(rows, heads, HEAD_DIM)
    key_heads = whole_keys.reshape(count, heads, HEAD_DIM)
    value_heads = whole_values.reshape(count, heads, HEAD_DIM)
    scores = (
        jnp.einsum("qhd,khd->hqk", query_heads, key_heads, preferred_element_type=jnp.float32)
        * scale
    )
    visible = key_pos[None, None, :] <= query_pos[None, :, None]
    top = jnp.max(jnp.where(visible, scores, -1e30), axis=2)
    weights = jnp.where(visible, jnp.exp(scores - top[:, :, None]), 0.0)
    total = jnp.sum(weights, axis=2)
    summed = jnp.einsum(
        "hqk,khd->hqd",
        weights.astype(jnp.bfloat16),
        value_heads,
        preferred_element_type=jnp.float32,
    )
    result = summed / total[:, :, None]
    attended = jnp.transpose(result, (1, 0, 2)).reshape(rows, width).astype(jnp.bfloat16)
    return lax.psum_scatter(
        jnp.dot(attended, w_out, preferred_element_type=jnp.float32).astype(jnp.bfloat16),
        "help",
        scatter_dimension=0,
        tiled=True,
    )


def column_spans(base, width):
    spans = []
    while width:
        lanes = width if width <= 384 else 256
        spans.append((base, lanes))
        base, width = base + lanes, width - lanes
    return tuple(spans)


def kernel(
    chips, rows, parts,
    bp_ref, q_hbm, k_hbm, v_hbm, w_hbm, out_ref,
    qbuf, kv, acc, top, total, qpos, osend, att_a, att_b, wbuf, part, psend, precv,
    own_sem, w_sem, q_send, q_recv, kv_send, kv_recv, relay_send, relay_recv,
    o_own, o_send, o_recv, p_send, p_recv,
):
    ctx = lax.axis_index("ctx")
    helper = lax.axis_index("help")
    chip = lax.div(ctx, 2)
    core = lax.rem(ctx, 2)
    sibling = chip * 2 + (1 - core)
    half = rows // 2
    size = (att_a.shape[0], att_b.shape[0])
    start = ((1 - helper) * size[1], helper * size[0])
    base = (0, chips * size[0])
    spans = tuple(column_spans(base[i], chips * size[i]) for i in range(2))
    att = (att_a, att_b)
    fold = math.log2(math.e) / HEAD_DIM**0.5

    def peer(step):
        found = 0
        for bit in range(chips.bit_length() - 1):
            mine = lax.rem(lax.div(chip, 1 << bit), 2)
            other = step // (1 << bit) % 2 if isinstance(step, int) else lax.rem(
                lax.div(step, 1 << bit), 2
            )
            found = found + (mine + other - 2 * mine * other) * (1 << bit)
        return found

    def head_of(ref, which):
        return ref.at[:, pl.ds(pl.multiple_of(which * HEAD_DIM, HEAD_DIM), HEAD_DIM)]

    def query_rows(which, head):
        return q_hbm.at[
            pl.ds(pl.multiple_of(start[which], 16), size[which]),
            pl.ds(pl.multiple_of(head * HEAD_DIM, HEAD_DIM), HEAD_DIM),
        ]

    def held_rows(ref, which, block):
        return ref.at[pl.ds(pl.multiple_of(base[which] + block * size[which], 16), size[which]), :]

    w_copy = pltpu.make_async_copy(w_hbm, wbuf, w_sem)
    own = [
        pltpu.make_async_copy(head_of(k_hbm, chip), kv.at[chip, core, 0], own_sem.at[0]),
        pltpu.make_async_copy(head_of(v_hbm, chip), kv.at[chip, core, 1], own_sem.at[1]),
        pltpu.make_async_copy(query_rows(0, chip), held_rows(qbuf, 0, chip), own_sem.at[2]),
        pltpu.make_async_copy(query_rows(1, chip), held_rows(qbuf, 1, chip), own_sem.at[3]),
    ]
    for copy in own:
        copy.start()

    barrier = pltpu.get_barrier_semaphore()
    for step in range(1, chips):
        pl.semaphore_signal(
            barrier, inc=1, device_id=(peer(step) * 2 + core, helper), device_id_type=MESH
        )
    pl.semaphore_signal(barrier, inc=1, device_id=(sibling, helper), device_id_type=MESH)
    pl.semaphore_signal(barrier, inc=1, device_id=(ctx, 1 - helper), device_id_type=MESH)
    pl.semaphore_wait(barrier, chips + 1)

    def q_copy(which, step, source):
        return pltpu.make_async_remote_copy(
            src_ref=query_rows(which, peer(step)),
            dst_ref=held_rows(qbuf, which, source),
            send_sem=q_send.at[which, step],
            recv_sem=q_recv.at[which, source],
            device_id=(peer(step) * 2 + core, helper),
            device_id_type=MESH,
        )

    def kv_copy(step, source, which):
        return pltpu.make_async_remote_copy(
            src_ref=head_of((k_hbm, v_hbm)[which], peer(step)),
            dst_ref=kv.at[source, core, which],
            send_sem=kv_send.at[step, which],
            recv_sem=kv_recv.at[source, which],
            device_id=(peer(step) * 2 + core, helper),
            device_id_type=MESH,
        )

    def relay(source, from_core):
        return pltpu.make_async_remote_copy(
            src_ref=kv.at[source, from_core],
            dst_ref=kv.at[source, from_core],
            send_sem=relay_send.at[source],
            recv_sem=relay_recv.at[source],
            device_id=(sibling, helper),
            device_id_type=MESH,
        )

    for step in range(1, chips):
        q_copy(0, step, chip).start()
    for step in range(1, chips):
        kv_copy(step, chip, 0).start()
        kv_copy(step, chip, 1).start()
    for step in range(1, chips):
        q_copy(1, step, chip).start()
    w_copy.start()

    lane = lax.broadcasted_iota(jnp.int32, qpos.shape, 1)
    position = jnp.zeros(qpos.shape, jnp.int32)
    for which in range(2):
        for block in range(chips):
            begin = base[which] + block * size[which]
            inside = (lane >= begin) & (lane < begin + size[which])
            place = bp_ref[block * 2 + core] * rows + start[which] - begin
            position = jnp.where(inside, lane + place, position)
    qpos[...] = position
    acc[...] = jnp.zeros_like(acc)
    total[...] = jnp.zeros_like(total)
    top[...] = jnp.full(top.shape, -1e9, jnp.float32)

    def attend(source, which):
        keys = kv[source, :, 0].reshape(2 * rows, HEAD_DIM)
        values = kv[source, :, 1].reshape(2 * rows, HEAD_DIM).T
        first = bp_ref[source * 2] * rows
        second = bp_ref[source * 2 + 1] * rows
        for begin, lanes in spans[which]:
            cols = pl.ds(begin, lanes)
            raw = lax.dot_general(
                keys, qbuf[cols, :], (((1,), (1,)), ((), ())), preferred_element_type=jnp.float32
            )
            inner = lax.broadcasted_iota(jnp.int32, (rows, lanes), 0)
            place = qpos[:, cols]
            raw = jnp.concatenate(
                [
                    jnp.where(inner <= place - first, raw[:rows], -1e30),
                    jnp.where(inner <= place - second, raw[rows:], -1e30),
                ],
                axis=0,
            )
            before = top[:, cols]
            after = jnp.maximum(before, jnp.max(raw, axis=0, keepdims=True))
            weights = jnp.exp2(raw * fold - after * fold)
            keep = jnp.exp2((before - after) * fold)
            top[:, cols] = after
            total[:, cols] = total[:, cols] * keep + jnp.sum(weights, axis=0, keepdims=True)
            acc[:, cols] = acc[:, cols] * keep + jnp.dot(
                values, weights.astype(jnp.bfloat16), preferred_element_type=jnp.float32
            )

    own[0].wait()
    own[1].wait()
    relay(chip, core).start()
    own[2].wait()
    for step in range(1, chips):
        q_copy(0, step, peer(step)).wait_recv()

    def turn(index):
        return index

    def one_step(index, carry):
        step = turn(index)
        source = peer(step)
        kv_copy(step, source, 0).wait_recv()
        kv_copy(step, source, 1).wait_recv()
        relay(source, core).start()
        done = lax.select(index == 1, chip, peer(turn(index - 1)))
        relay(done, 1 - core).wait_recv()
        attend(done, 0)
        return carry

    lax.fori_loop(1, chips, one_step, 0)
    last = peer(turn(chips - 1))
    relay(last, 1 - core).wait_recv()
    attend(last, 0)

    def o_copy(which, step, head):
        return pltpu.make_async_remote_copy(
            src_ref=held_rows(osend, which, peer(step)),
            dst_ref=head_of(att[which], head),
            send_sem=o_send.at[which, step],
            recv_sem=o_recv.at[which, head],
            device_id=(peer(step) * 2 + core, helper),
            device_id_type=MESH,
        )

    def o_local(which):
        return pltpu.make_async_copy(
            held_rows(osend, which, chip), head_of(att[which], chip), o_own.at[which]
        )

    def give(which):
        for begin, lanes in spans[which]:
            cols = pl.ds(begin, lanes)
            result = acc[:, cols] * (1.0 / total[:, cols])
            osend[cols, :] = result.T.astype(jnp.bfloat16)
        for step in range(1, chips):
            o_copy(which, step, chip).start()
        o_local(which).start()

    def take(which):
        o_local(which).wait()
        for step in range(1, chips):
            o_copy(which, step, peer(step)).wait_recv()

    give(0)
    own[3].wait()
    for step in range(1, chips):
        q_copy(1, step, peer(step)).wait_recv()

    def second_pass(source, carry):
        attend(source, 1)
        return carry

    lax.fori_loop(0, chips, second_pass, 0)
    give(1)

    wide = w_hbm.shape[1] // parts

    def p_copy(index):
        return pltpu.make_async_remote_copy(
            src_ref=psend.at[index],
            dst_ref=precv.at[index],
            send_sem=p_send.at[index],
            recv_sem=p_recv.at[index],
            device_id=(ctx, 1 - helper),
            device_id_type=MESH,
        )

    w_copy.wait()
    take(0)
    for index in range(parts):
        cols = pl.ds(index * wide, wide)
        product = jnp.dot(att_a[...], wbuf[:, cols], preferred_element_type=jnp.float32)
        part[:, cols] = product
        psend[index] = product.astype(jnp.bfloat16)
        p_copy(index).start()
    take(1)
    spare = size[0] - half
    for index in range(parts):
        cols = pl.ds(index * wide, wide)
        product = jnp.dot(att_b[...], wbuf[:, cols], preferred_element_type=jnp.float32)
        mine = jnp.where(
            helper == 0,
            jnp.concatenate([product, part[:spare, cols]], axis=0),
            jnp.concatenate([part[half:, cols], product], axis=0),
        )
        p_copy(index).wait_recv()
        theirs = precv[index].astype(jnp.float32)
        theirs = jnp.where(helper == 0, theirs[:half], theirs[spare:])
        out_ref[:, cols] = (mine + theirs).astype(jnp.bfloat16)

    for step in range(1, chips):
        for which in range(2):
            q_copy(which, step, chip).wait_send()
            kv_copy(step, chip, which).wait_send()
            o_copy(which, step, chip).wait_send()
    for source in range(chips):
        relay(source, core).wait_send()
    for index in range(parts):
        p_copy(index).wait_send()


def exchanged_body(chips, queries, keys, values, block_pos, w_out):
    rows, width = queries.shape
    out_width = w_out.shape[1]
    count = chips * rows
    parts = 4
    first = -(-(rows // 2) // 16) * 16
    bf16, f32 = jnp.bfloat16, jnp.float32
    dma = pltpu.SemaphoreType.DMA
    anywhere = pl.BlockSpec(memory_space=pltpu.HBM)
    return pl.pallas_call(
        functools.partial(kernel, chips, rows, parts),
        out_shape=jax.ShapeDtypeStruct((rows // 2, out_width), bf16),
        in_specs=[pl.BlockSpec(memory_space=pltpu.SMEM)] + [anywhere] * 4,
        out_specs=pl.BlockSpec(memory_space=pltpu.VMEM),
        scratch_shapes=[
            pltpu.VMEM((count, HEAD_DIM), bf16),
            pltpu.VMEM((chips, 2, 2, rows, HEAD_DIM), bf16),
            pltpu.VMEM((HEAD_DIM, count), f32),
            pltpu.VMEM((1, count), f32),
            pltpu.VMEM((1, count), f32),
            pltpu.VMEM((1, count), jnp.int32),
            pltpu.VMEM((count, HEAD_DIM), bf16),
            pltpu.VMEM((first, width), bf16),
            pltpu.VMEM((rows - first, width), bf16),
            pltpu.VMEM((width, out_width), bf16),
            pltpu.VMEM((first, out_width), f32),
            pltpu.VMEM((parts, first, out_width // parts), bf16),
            pltpu.VMEM((parts, first, out_width // parts), bf16),
            dma((4,)),
            dma,
            dma((2, chips)),
            dma((2, chips)),
            dma((chips, 2)),
            dma((chips, 2)),
            dma((chips,)),
            dma((chips,)),
            dma((2,)),
            dma((2, chips)),
            dma((2, chips)),
            dma((parts,)),
            dma((parts,)),
        ],
        compiler_params=pltpu.CompilerParams(
            collective_id=0, has_side_effects=True, vmem_limit_bytes=60 * 1024 * 1024
        ),
        cost_estimate=pl.CostEstimate(
            flops=8 * count * count * HEAD_DIM + 2 * rows * width * out_width,
            bytes_accessed=2 * (3 * rows * width + width * out_width),
            transcendentals=2 * count * count,
        ),
        name="exchange_attend_project",
    )(block_pos, queries, keys, values, w_out)


def solution(mesh):
    chips = mesh.shape["ctx"] // 2

    def body(queries, keys, values, block_pos, w_out):
        fits = mesh.shape["help"] == 2 and queries.shape[1] == chips * HEAD_DIM
        if fits and chips & (chips - 1) == 0 and queries.shape[0] % 16 == 0:
            return exchanged_body(chips, queries, keys, values, block_pos, w_out)
        return gathered_body(queries, keys, values, block_pos, w_out)

    in_specs = (P("ctx", "help"), P("ctx", "help"), P("ctx", "help"), P(), P("help", None))
    out_specs = P(("ctx", "help"), None)
    return jax.shard_map(body, mesh=mesh, in_specs=in_specs, out_specs=out_specs, check_vma=False)
```

time: 58 us -> 47.5 us (0.82)
  Pallas kernels: 51.3 us -> 45.7 us
  local copies, waits for them, and re-layouts: 6.44 us -> 1.69 us
    pallas_call x1, Pallas kernels: 51.3 us -> 45.7 us  [exchanged_body(): pl.pallas_call(functools.partial(kernel, chips, rows, parts), out_shape=j...]
    unnamed x11 -> x1, local copies, waits for them, and re-layouts: 6.44 us -> 1.69 us
where the time goes in v2:
time: 47.5 us; the launch traced here: 47.4 us
  Pallas kernels  45.7 us (96%)
  local copies, waits for them, and re-layouts  1.69 us (4%)
    pallas_call x1, Pallas kernels, exchanged_body(): pl.pallas_call(functools.partial(kernel, chips, rows, parts), out_shape=j...  45.7 us
    unnamed x1, local copies, waits for them, and re-layouts  1.69 us

profile of v2, /device:TPU:0, one launch (start us, length us, event | category | flops | bytes accessed | tf_op | source)
XLA Modules:
  0.0 47.4 jit_solution(12084710923549671223)
XLA Ops:
  0.0 45.7 %exchange_attend_project.1 = bf16[72,2048]{1,0:T(8,128)(2,1)} custom-call(s32[16]{0:T(128)} %bp_ref.1, bf16[144,1024]{1,0:T(8,128)(2,1)} %q_hbm.1, bf16[144,1024]{1,0:T(8,128)(2,1)} %k_hbm.1, bf16[144,1024]{1,0:T(8,128)(2,1)} %v_hbm.1, bf16[1024,2048]{1,0:T(8,128)(2,1)} %w_hbm.1), custom_call_target="tpu_custom_call" | custom-call | flops 1962934272 | bytes 5079040 | tf_op jit(solution)/shard_map/exchange_attend_project/pallas_call | solution.py:327
  45.7 1.7 %copy.7 = bf16[72,2048]{1,0:T(8,128)(2,1)} copy(bf16[72,2048]{1,0:T(8,128)(2,1)} %exchange_attend_project.1) | data formatting | bytes 589824

commit v3 on v2

--- a/solution.py
+++ b/solution.py
@@ -63,7 +63,8 @@
 def kernel(
     chips, rows, parts,
     bp_ref, q_hbm, k_hbm, v_hbm, w_hbm, out_ref,
-    qbuf, kv, acc, top, total, qpos, osend, att_a, att_b, wbuf, part, psend, precv,
+    qbuf, kv, acc, top, total, qpos, osend, att_a, att_b, att_c, wbuf, part,
+    psend_a, psend_b, precv_a, precv_b,
     own_sem, w_sem, q_send, q_recv, kv_send, kv_recv, relay_send, relay_recv,
     o_own, o_send, o_recv, p_send, p_recv,
 ):
@@ -73,11 +74,14 @@
     core = lax.rem(ctx, 2)
     sibling = chip * 2 + (1 - core)
     half = rows // 2
-    size = (att_a.shape[0], att_b.shape[0])
-    start = ((1 - helper) * size[1], helper * size[0])
-    base = (0, chips * size[0])
-    spans = tuple(column_spans(base[i], chips * size[i]) for i in range(2))
-    att = (att_a, att_b)
+    att = (att_a, att_b, att_c)
+    sets = range(3)
+    size = tuple(ref.shape[0] for ref in att)
+    swapped = size[0] + size[1]
+    start = ((1 - helper) * size[2], (1 - helper) * size[2] + size[0], helper * swapped)
+    base = (0, chips * size[0], chips * swapped)
+    spans = tuple(column_spans(base[i], chips * size[i]) for i in sets)
+    psend, precv = (psend_a, psend_b), (precv_a, precv_b)
     fold = math.log2(math.e) / HEAD_DIM**0.5
 
     def peer(step):
@@ -106,11 +110,13 @@
     own = [
         pltpu.make_async_copy(head_of(k_hbm, chip), kv.at[chip, core, 0], own_sem.at[0]),
         pltpu.make_async_copy(head_of(v_hbm, chip), kv.at[chip, core, 1], own_sem.at[1]),
-        pltpu.make_async_copy(query_rows(0, chip), held_rows(qbuf, 0, chip), own_sem.at[2]),
-        pltpu.make_async_copy(query_rows(1, chip), held_rows(qbuf, 1, chip), own_sem.at[3]),
+    ] + [
+        pltpu.make_async_copy(query_rows(i, chip), held_rows(qbuf, i, chip), own_sem.at[2 + i])
+        for i in sets
     ]
     for copy in own:
         copy.start()
+    w_copy.start()
 
     barrier = pltpu.get_barrier_semaphore()
     for step in range(1, chips):
@@ -152,17 +158,17 @@
         )
 
     for step in range(1, chips):
-        q_copy(0, step, chip).start()
+        for which in (0, 1):
+            q_copy(which, step, chip).start()
     for step in range(1, chips):
         kv_copy(step, chip, 0).start()
         kv_copy(step, chip, 1).start()
     for step in range(1, chips):
-        q_copy(1, step, chip).start()
-    w_copy.start()
+        q_copy(2, step, chip).start()
 
     lane = lax.broadcasted_iota(jnp.int32, qpos.shape, 1)
     position = jnp.zeros(qpos.shape, jnp.int32)
-    for which in range(2):
+    for which in sets:
         for block in range(chips):
             begin = base[which] + block * size[which]
             inside = (lane >= begin) & (lane < begin + size[which])
@@ -173,12 +179,12 @@
     total[...] = jnp.zeros_like(total)
     top[...] = jnp.full(top.shape, -1e9, jnp.float32)
 
-    def attend(source, which):
+    def attend(source, chosen):
         keys = kv[source, :, 0].reshape(2 * rows, HEAD_DIM)
         values = kv[source, :, 1].reshape(2 * rows, HEAD_DIM).T
         first = bp_ref[source * 2] * rows
         second = bp_ref[source * 2 + 1] * rows
-        for begin, lanes in spans[which]:
+        for begin, lanes in sum((spans[i] for i in chosen), ()):
             cols = pl.ds(begin, lanes)
             raw = lax.dot_general(
                 keys, qbuf[cols, :], (((1,), (1,)), ((), ())), preferred_element_type=jnp.float32
@@ -205,9 +211,13 @@
     own[0].wait()
     own[1].wait()
     relay(chip, core).start()
-    own[2].wait()
-    for step in range(1, chips):
-        q_copy(0, step, peer(step)).wait_recv()
+    def take_queries(which):
+        own[2 + which].wait()
+        for step in range(1, chips):
+            q_copy(which, step, peer(step)).wait_recv()
+
+    take_queries(0)
+    take_queries(1)
 
     def turn(index):
         return index
@@ -220,13 +230,12 @@
         relay(source, core).start()
         done = lax.select(index == 1, chip, peer(turn(index - 1)))
         relay(done, 1 - core).wait_recv()
-        attend(done, 0)
+        attend(done, (0, 1))
         return carry
 
     lax.fori_loop(1, chips, one_step, 0)
     last = peer(turn(chips - 1))
     relay(last, 1 - core).wait_recv()
-    attend(last, 0)
 
     def o_copy(which, step, head):
         return pltpu.make_async_remote_copy(
@@ -257,70 +266,87 @@
         for step in range(1, chips):
             o_copy(which, step, peer(step)).wait_recv()
 
-    give(0)
-    own[3].wait()
-    for step in range(1, chips):
-        q_copy(1, step, peer(step)).wait_recv()
+    for which in range(2):
+        attend(last, (which,))
+        give(which)
 
     def second_pass(source, carry):
-        attend(source, 1)
+        attend(source, (2,))
         return carry
 
-    lax.fori_loop(0, chips, second_pass, 0)
-    give(1)
-
     wide = w_hbm.shape[1] // parts
 
-    def p_copy(index):
+    def p_copy(which, index):
         return pltpu.make_async_remote_copy(
-            src_ref=psend.at[index],
-            dst_ref=precv.at[index],
-            send_sem=p_send.at[index],
-            recv_sem=p_recv.at[index],
+            src_ref=psend[which].at[index],
+            dst_ref=precv[which].at[index],
+            send_sem=p_send.at[which, index],
+            recv_sem=p_recv.at[which, index],
             device_id=(ctx, 1 - helper),
             device_id_type=MESH,
         )
 
+    def project_early(which):
+        take(which)
+        held = pl.ds(which * size[0], size[which])
+        for index in range(parts):
+            cols = pl.ds(index * wide, wide)
+            product = jnp.dot(att[which][...], wbuf[:, cols], preferred_element_type=jnp.float32)
+            part[held, cols] = product
+            psend[which][index] = product.astype(jnp.bfloat16)
+            p_copy(which, index).start()
+
     w_copy.wait()
-    take(0)
+    take_queries(2)
+    cut = chips // 2
+    lax.fori_loop(0, cut, second_pass, 0)
+    if cut < chips:
+        project_early(0)
+        lax.fori_loop(cut, chips, second_pass, 0)
+    give(2)
+    if cut == chips:
+        project_early(0)
+    project_early(1)
+    take(2)
+    spare = swapped - half
     for index in range(parts):
         cols = pl.ds(index * wide, wide)
-        product = jnp.dot(att_a[...], wbuf[:, cols], preferred_element_type=jnp.float32)
-        part[:, cols] = product
-        psend[index] = product.astype(jnp.bfloat16)
-        p_copy(index).start()
-    take(1)
-    spare = size[0] - half
-    for index in range(parts):
-        cols = pl.ds(index * wide, wide)
-        product = jnp.dot(att_b[...], wbuf[:, cols], preferred_element_type=jnp.float32)
-        mine = jnp.where(
+        product = jnp.dot(att_c[...], wbuf[:, cols], preferred_element_type=jnp.float32)
+        part[:half, cols] = jnp.where(
             helper == 0,
             jnp.concatenate([product, part[:spare, cols]], axis=0),
             jnp.concatenate([part[half:, cols], product], axis=0),
         )
-        p_copy(index).wait_recv()
-        theirs = precv[index].astype(jnp.float32)
+    for index in range(parts):
+        cols = pl.ds(index * wide, wide)
+        for which in range(2):
+            p_copy(which, index).wait_recv()
+        theirs = jnp.concatenate(
+            [precv[i][index].astype(jnp.float32) for i in range(2)], axis=0
+        )
         theirs = jnp.where(helper == 0, theirs[:half], theirs[spare:])
-        out_ref[:, cols] = (mine + theirs).astype(jnp.bfloat16)
+        out_ref[:, cols] = (part[:half, cols] + theirs).astype(jnp.bfloat16)
 
     for step in range(1, chips):
+        for which in sets:
+            q_copy(which, step, chip).wait_send()
+            o_copy(which, step, chip).wait_send()
         for which in range(2):
-            q_copy(which, step, chip).wait_send()
             kv_copy(step, chip, which).wait_send()
-            o_copy(which, step, chip).wait_send()
     for source in range(chips):
         relay(source, core).wait_send()
-    for index in range(parts):
-        p_copy(index).wait_send()
+    for which in range(2):
+        for index in range(parts):
+            p_copy(which, index).wait_send()
 
 
 def exchanged_body(chips, queries, keys, values, block_pos, w_out):
     rows, width = queries.shape
     out_width = w_out.shape[1]
     count = chips * rows
-    parts = 4
+    parts = 2
     first = -(-(rows // 2) // 16) * 16
+    early = 48
     bf16, f32 = jnp.bfloat16, jnp.float32
     dma = pltpu.SemaphoreType.DMA
     anywhere = pl.BlockSpec(memory_space=pltpu.HBM)
@@ -337,25 +363,28 @@
             pltpu.VMEM((1, count), f32),
             pltpu.VMEM((1, count), jnp.int32),
             pltpu.VMEM((count, HEAD_DIM), bf16),
-            pltpu.VMEM((first, width), bf16),
+            pltpu.VMEM((early, width), bf16),
+            pltpu.VMEM((first - early, width), bf16),
             pltpu.VMEM((rows - first, width), bf16),
             pltpu.VMEM((width, out_width), bf16),
             pltpu.VMEM((first, out_width), f32),
-            pltpu.VMEM((parts, first, out_width // parts), bf16),
-            pltpu.VMEM((parts, first, out_width // parts), bf16),
-            dma((4,)),
+            pltpu.VMEM((parts, early, out_width // parts), bf16),
+            pltpu.VMEM((parts, first - early, out_width // parts), bf16),
+            pltpu.VMEM((parts, early, out_width // parts), bf16),
+            pltpu.VMEM((parts, first - early, out_width // parts), bf16),
+            dma((5,)),
             dma,
-            dma((2, chips)),
-            dma((2, chips)),
+            dma((3, chips)),
+            dma((3, chips)),
             dma((chips, 2)),
             dma((chips, 2)),
             dma((chips,)),
             dma((chips,)),
-            dma((2,)),
-            dma((2, chips)),
-            dma((2, chips)),
-            dma((parts,)),
-            dma((parts,)),
+            dma((3,)),
+            dma((3, chips)),
+            dma((3, chips)),
+            dma((2, parts)),
+            dma((2, parts)),
         ],
         compiler_params=pltpu.CompilerParams(
             collective_id=0, has_side_effects=True, vmem_limit_bytes=60 * 1024 * 1024

time: 47.5 us -> 47 us (0.989)
  Pallas kernels: 45.7 us -> 45.2 us
    pallas_call x1, Pallas kernels: 45.7 us -> 45.2 us  [exchanged_body(): pl.pallas_call(functools.partial(kernel, chips, rows, parts), out_shape=j...]
where the time goes in v3:
time: 47 us; the launch traced here: 46.9 us
  Pallas kernels  45.2 us (96%)
  local copies, waits for them, and re-layouts  1.69 us (4%)
    pallas_call x1, Pallas kernels, exchanged_body(): pl.pallas_call(functools.partial(kernel, chips, rows, parts), out_shape=j...  45.2 us
    unnamed x1, local copies, waits for them, and re-layouts  1.69 us

profile of v3, /device:TPU:0, one launch (start us, length us, event | category | flops | bytes accessed | tf_op | source)
XLA Modules:
  0.0 46.9 jit_solution(9820643022533636594)
XLA Ops:
  0.0 45.2 %exchange_attend_project.1 = bf16[72,2048]{1,0:T(8,128)(2,1)} custom-call(s32[16]{0:T(128)} %bp_ref.1, bf16[144,1024]{1,0:T(8,128)(2,1)} %q_hbm.1, bf16[144,1024]{1,0:T(8,128)(2,1)} %k_hbm.1, bf16[144,1024]{1,0:T(8,128)(2,1)} %v_hbm.1, bf16[1024,2048]{1,0:T(8,128)(2,1)} %w_hbm.1), custom_call_target="tpu_custom_call" | custom-call | flops 1962934272 | bytes 5079040 | tf_op jit(solution)/shard_map/exchange_attend_project/pallas_call | solution.py:353
  45.2 1.7 %copy.7 = bf16[72,2048]{1,0:T(8,128)(2,1)} copy(bf16[72,2048]{1,0:T(8,128)(2,1)} %exchange_attend_project.1) | data formatting | bytes 589824

commit v4 on v3

--- a/solution.py
+++ b/solution.py
@@ -163,8 +163,6 @@
     for step in range(1, chips):
         kv_copy(step, chip, 0).start()
         kv_copy(step, chip, 1).start()
-    for step in range(1, chips):
-        q_copy(2, step, chip).start()
 
     lane = lax.broadcasted_iota(jnp.int32, qpos.shape, 1)
     position = jnp.zeros(qpos.shape, jnp.int32)
@@ -233,7 +231,10 @@
         attend(done, (0, 1))
         return carry
 
-    lax.fori_loop(1, chips, one_step, 0)
+    lax.fori_loop(1, chips - 2, one_step, 0)
+    for step in range(1, chips):
+        q_copy(2, step, chip).start()
+    lax.fori_loop(chips - 2, chips, one_step, 0)
     last = peer(turn(chips - 1))
     relay(last, 1 - core).wait_recv()
 

time: 47 us -> 46.3 us (0.985)
  Pallas kernels: 45.2 us -> 44.5 us
    pallas_call x1, Pallas kernels: 45.2 us -> 44.5 us  [exchanged_body(): pl.pallas_call(functools.partial(kernel, chips, rows, parts), out_shape=j...]
where the time goes in v4:
time: 46.3 us; the launch traced here: 46.2 us
  Pallas kernels  44.5 us (96%)
  local copies, waits for them, and re-layouts  1.69 us (4%)
    pallas_call x1, Pallas kernels, exchanged_body(): pl.pallas_call(functools.partial(kernel, chips, rows, parts), out_shape=j...  44.5 us
    unnamed x1, local copies, waits for them, and re-layouts  1.69 us

profile of v4, /device:TPU:0, one launch (start us, length us, event | category | flops | bytes accessed | tf_op | source)
XLA Modules:
  0.0 46.2 jit_solution(12861343746314501411)
XLA Ops:
  0.0 44.5 %exchange_attend_project.1 = bf16[72,2048]{1,0:T(8,128)(2,1)} custom-call(s32[16]{0:T(128)} %bp_ref.1, bf16[144,1024]{1,0:T(8,128)(2,1)} %q_hbm.1, bf16[144,1024]{1,0:T(8,128)(2,1)} %k_hbm.1, bf16[144,1024]{1,0:T(8,128)(2,1)} %v_hbm.1, bf16[1024,2048]{1,0:T(8,128)(2,1)} %w_hbm.1), custom_call_target="tpu_custom_call" | custom-call | flops 1962934272 | bytes 5079040 | tf_op jit(solution)/shard_map/exchange_attend_project/pallas_call | solution.py:354
  44.5 1.7 %copy.7 = bf16[72,2048]{1,0:T(8,128)(2,1)} copy(bf16[72,2048]{1,0:T(8,128)(2,1)} %exchange_attend_project.1) | data formatting | bytes 589824

commit v5 on v4

--- a/solution.py
+++ b/solution.py
@@ -160,7 +160,7 @@
     for step in range(1, chips):
         for which in (0, 1):
             q_copy(which, step, chip).start()
-    for step in range(1, chips):
+    for step in [*range(chips // 2, chips), *range(1, chips // 2)]:
         kv_copy(step, chip, 0).start()
         kv_copy(step, chip, 1).start()
 

time: 46.3 us -> 46 us (level)
  no operation moved by 1% of the time
where the time goes in v5:
time: 46 us; the launch traced here: 45.8 us
  Pallas kernels  44.1 us (96%)
  local copies, waits for them, and re-layouts  1.69 us (4%)
    pallas_call x1, Pallas kernels, exchanged_body(): pl.pallas_call(functools.partial(kernel, chips, rows, parts), out_shape=j...  44.1 us
    unnamed x1, local copies, waits for them, and re-layouts  1.69 us

profile of v5, /device:TPU:0, one launch (start us, length us, event | category | flops | bytes accessed | tf_op | source)
XLA Modules:
  0.0 45.8 jit_solution(17785877409921006474)
XLA Ops:
  0.0 44.1 %exchange_attend_project.1 = bf16[72,2048]{1,0:T(8,128)(2,1)} custom-call(s32[16]{0:T(128)} %bp_ref.1, bf16[144,1024]{1,0:T(8,128)(2,1)} %q_hbm.1, bf16[144,1024]{1,0:T(8,128)(2,1)} %k_hbm.1, bf16[144,1024]{1,0:T(8,128)(2,1)} %v_hbm.1, bf16[1024,2048]{1,0:T(8,128)(2,1)} %w_hbm.1), custom_call_target="tpu_custom_call" | custom-call | flops 1962934272 | bytes 5079040 | tf_op jit(solution)/shard_map/exchange_attend_project/pallas_call | solution.py:354
  44.2 1.7 %copy.7 = bf16[72,2048]{1,0:T(8,128)(2,1)} copy(bf16[72,2048]{1,0:T(8,128)(2,1)} %exchange_attend_project.1) | data formatting | bytes 589824
